TPU v7x, 32 devices: a whole 2x2x4 slice. The times are simulated.
32 devices in a mesh: node: 2 (over x), row: 16 (over z, y, core).
Axes of the slice: x: 2, y: 2, z: 4, core: 2. Of those that a mesh axis runs over, the one named last changes fastest.
Arguments:
- leaves: float32 [4, 8192, 256], P('node', 'row'), may hold values from -200 to 200
- level_one: float32 [2, 256, 256, 256], P('node', 'row'), may hold values from -20 to 20
- level_two: float32 [2, 128, 256, 256], P('node', 'row'), may hold values from -20 to 20
Outputs:
- leaf_bases: float32 [4, 8192, 256], P('node', 'row')
- level_one_bases: float32 [2, 256, 256, 256], P('node', None, 'row')
- level_two_bases: float32 [2, 128, 256, 256], P('node', None, 'row')
- level_two_factors: float32 [2, 256, 256], P('node')
All inputs are finite; a program needn't handle non-finite values.
Results may differ from a plain program's by a relative error of at most 0.0003.
Values sent between devices are 32-bit elements; how exact they have to be, the bound alone decides.
No kernel may reach another device: no remote copies, remote signals or barrier semaphores. Data moves between devices by JAX's collectives and lax.ppermute only.
A program may use at most 64 MiB of HBM per device.

v0:
```python
import jax
import jax.numpy as jnp
from jax import lax
from jax.sharding import PartitionSpec as P

PRECISE = lax.Precision.HIGHEST


def swapped(value, axis, stride):
    mask = 2**stride
    pairs = [(source, source ^ mask) for source in range(lax.axis_size(axis))]
    return lax.ppermute(value, axis, pairs)


def factored(gram_matrix):
    width = gram_matrix.shape[-1]
    lower = jnp.linalg.cholesky(gram_matrix)
    identity = jnp.eye(width, dtype=gram_matrix.dtype)
    inverse_lower = jax.scipy.linalg.solve_triangular(lower, identity, lower=True)
    return (lower.T, inverse_lower.T)


def body(leaves, level_one, level_two):
    rows_total = leaves.shape[1] * lax.axis_size("row")
    leaf_grams = jnp.einsum("nrc,nrd->ncd", leaves, leaves, precision=PRECISE)
    leaf_grams = lax.psum(leaf_grams, "row") / rows_total
    leaf_upper, leaf_inverse = jax.vmap(factored)(leaf_grams)
    leaf_bases = jnp.einsum("nrc,ncd->nrd", leaves, leaf_inverse, precision=PRECISE)
    slab_rows = level_one[0]
    rank_width = slab_rows.shape[1]
    turned = jnp.einsum("jb,ibk->ijk", leaf_upper[1], slab_rows, precision=PRECISE)
    moved_one = jnp.einsum(
        "ia,ajk->ijk",
        leaf_upper[0],
        lax.all_to_all(turned, "row", split_axis=1, concat_axis=0, tiled=True),
        precision=PRECISE,
    )
    flat_one = moved_one.reshape(-1, rank_width)
    one_gram = jnp.dot(flat_one.T, flat_one, precision=PRECISE, preferred_element_type=jnp.float32)
    one_gram = lax.psum(one_gram, "row") / (rank_width * rank_width)
    one_upper, one_inverse = factored(one_gram)
    level_one_bases = jnp.dot(
        flat_one, one_inverse, precision=PRECISE, preferred_element_type=jnp.float32
    )
    level_one_bases = level_one_bases.reshape(moved_one.shape)[None]
    partner = swapped(one_upper, "node", 0)
    is_left = lax.axis_index("node") % 2 == 0
    left_factor = jnp.where(is_left, one_upper, partner)
    right_factor = jnp.where(is_left, partner, one_upper)
    half_slab = level_two[0]
    turned_two = jnp.einsum("jb,abk->ajk", right_factor, half_slab, precision=PRECISE)
    gathered = lax.all_to_all(turned_two, "row", split_axis=1, concat_axis=0, tiled=True)
    half_rows = gathered.shape[0]
    block_cols = gathered.shape[1]
    columns_split = left_factor.reshape(rank_width, half_rows, 2)
    own_columns = jnp.where(is_left, columns_split[:, :, 0], columns_split[:, :, 1])
    partial_sum = jnp.einsum("ia,ajk->ijk", own_columns, gathered, precision=PRECISE)
    split_sum = partial_sum.reshape(half_rows, 2, block_cols, rank_width)
    keep_part = jnp.where(is_left, split_sum[:, 0], split_sum[:, 1])
    send_part = jnp.where(is_left, split_sum[:, 1], split_sum[:, 0])
    moved_two = keep_part + swapped(send_part, "node", 0)
    flat_two = moved_two.reshape(-1, rank_width)
    two_gram = jnp.dot(flat_two.T, flat_two, precision=PRECISE, preferred_element_type=jnp.float32)
    row_total = lax.psum(two_gram, "row")
    two_gram = row_total + swapped(row_total, "node", 0)
    two_gram = two_gram / (rank_width * rank_width)
    two_upper, two_inverse = factored(two_gram)
    level_two_bases = jnp.dot(
        flat_two, two_inverse, precision=PRECISE, preferred_element_type=jnp.float32
    )
    level_two_bases = level_two_bases.reshape(moved_two.shape)[None]
    return (leaf_bases, level_one_bases, level_two_bases, two_upper[None])


def solution(mesh):
    placed = (P("node", "row", None), P("node", "row", None, None), P("node", "row", None, None))
    return jax.shard_map(
        body,
        mesh=mesh,
        in_specs=placed,
        out_specs=(
            P("node", "row", None),
            P("node", None, "row", None),
            P("node", None, "row", None),
            P("node", None, None),
        ),
        check_vma=False,
    )
```

profile of v0, /device:TPU:0, one launch (start us, length us, event | category | flops | bytes accessed | tf_op | source)
XLA Modules:
  0.0 734.2 jit_solution(13152481969509227665)
XLA Ops:
  7.2 4.3 fusion.64
  11.7 93.2 %all-reduce.6.cloned.1.call-done = f32[2,256,256]{1,2,0:T(8,128)} async-done(((f32[2,256,256]{1,2,0:T(8,128)}), f32[2,256,256]{1,2,0:T(8,128)}) %all-reduce.6.cloned.1.call-update) | async-done | bytes 524304 | tf_op jit(solution)/shard_map/psum | solution.py:26
  104.9 1.9 broadcast_multiply_fusion
  109.0 23.5 %custom-call.28 = f32[2,128,128]{2,1,0:T(8,128)S(1)} custom-call(f32[2,128,128]{2,1,0:T(8,128)S(1)} %cholesky.316), custom_call_target="Cholesky" | custom-call | tf_op jit(solution)/shard_map/vmap(jit(cholesky))/cholesky | solution.py:17
  132.5 19.7 %custom-call.29 = f32[2,1,128,128]{2,3,1,0:T(8,128)S(1)} custom-call(f32[2,1,128,128]{3,2,1,0:T(8,128)S(1)} %select_bitcast_fusion.1), custom_call_target="InvertDiagBlocksLowerTriangular" | custom-call | tf_op jit(solution)/shard_map/vmap(jit(cholesky))/cholesky | solution.py:17
  154.7 23.5 %custom-call.30 = f32[2,128,128]{2,1,0:T(8,128)S(1)} custom-call(f32[2,128,128]{2,1,0:T(8,128)S(1)} %convolution_subtract_fusion.3), custom_call_target="Cholesky" | custom-call | tf_op jit(solution)/shard_map/vmap(jit(cholesky))/cholesky | solution.py:17
  178.5 5.8 fusion.2
  184.3 2.4 copy.91
  186.7 97.3 %all_to_all.36 = f32[16,256,256]{2,0,1:T(8,128)S(1)} all-to-all(f32[16,256,256]{2,0,1:T(8,128)S(1)} %copy.91), channel_id=1, replica_groups=mesh['node'=2,'row'=16] {'row'}, dimensions={1} | all-to-all | bytes 8388608 | tf_op jit(solution)/shard_map/all_to_all | solution.py:35
  284.6 3.8 fusion.19
  288.4 2.0 copy-done.2
  290.4 7.4 %convolution_bitcast_fusion.3 = f32[256,256]{0,1:T(8,128)} fusion(f32[256,16,256]{2,0,1:T(8,128)S(1)} %fusion.19), kind=kOutput, calls=%fused_computation.20 | convolution fusion | flops 3221225472 | bytes 4456448 | tf_op jit(solution)/shard_map/dot_general | solution.py:39
  297.9 89.5 %all-reduce.8.cloned.1.call-done = f32[256,256]{0,1:T(8,128)} async-done(((f32[256,256]{0,1:T(8,128)}), f32[256,256]{0,1:T(8,128)}) %all-reduce.8.cloned.1.call-update) | async-done | bytes 262160 | tf_op jit(solution)/shard_map/psum | solution.py:40
  389.5 11.9 %cholesky.252 = f32[128,128]{1,0:T(8,128)S(1)} custom-call(f32[128,128]{1,0:T(8,128)S(1)} %cholesky.319), custom_call_target="Cholesky" | custom-call | tf_op jit(solution)/shard_map/jit(cholesky)/cholesky | solution.py:17
  401.5 9.8 %custom-call.34 = f32[1,128,128]{1,2,0:T(8,128)S(1)} custom-call(f32[1,128,128]{2,1,0:T(8,128)S(1)} %get-tuple-element.96), custom_call_target="InvertDiagBlocksLowerTriangular" | custom-call | tf_op jit(solution)/shard_map/jit(cholesky)/cholesky | solution.py:17
  411.8 11.7 %cholesky.269 = f32[128,128]{1,0:T(8,128)S(1)} custom-call(f32[128,128]{1,0:T(8,128)S(1)} %convolution_subtract_fusion.5), custom_call_target="Cholesky" | custom-call | tf_op jit(solution)/shard_map/jit(cholesky)/cholesky | solution.py:17
  426.1 1.5 collective-permute-start
  427.7 7.3 collective-permute-done
  435.0 1.9 fusion.10
  436.9 2.9 copy.100
  439.8 3.7 all-to-all-start.1
  444.5 5.6 while.5
  445.1 2.1 bitcast_dynamic-update-slice_fusion.6
  448.0 2.1 bitcast_dynamic-update-slice_fusion.6
  450.1 40.8 %custom-call.31 = f32[2,2,128,128]{2,3,1,0:T(8,128)} custom-call(f32[2,2,128,128]{3,2,1,0:T(8,128)} %bitcast.184), custom_call_target="InvertDiagBlocksLowerTriangular" | custom-call | tf_op jit(solution)/shard_map/vmap(jit(_solve_triangular))/triangular_solve | solution.py:19
  494.7 3.6 fusion.5
  498.3 1.6 select_bitcast_fusion
  500.8 2.4 collective-permute-start.1
  506.9 4.0 while.6
  507.5 1.4 bitcast_dynamic-update-slice_fusion.7
  509.5 1.4 bitcast_dynamic-update-slice_fusion.7
  510.9 19.8 %custom-call.35 = f32[2,128,128]{1,2,0:T(8,128)S(1)} custom-call(f32[2,128,128]{2,1,0:T(8,128)S(1)} %get-tuple-element.28), custom_call_target="InvertDiagBlocksLowerTriangular" | custom-call | tf_op jit(solution)/shard_map/jit(_solve_triangular)/triangular_solve | solution.py:19
  531.3 18.5 %collective-permute-done.1 = f32[128,16,256]{2,0,1:T(8,128)} collective-permute-done((f32[128,16,256]{2,0,1:T(8,128)}, f32[128,16,256]{2,0,1:T(8,128)}, u32[]{:S(2)}, u32[]{:S(2)}) %collective-permute-start.1) | collective-permute-done | bytes 2097184 | tf_op jit(solution)/shard_map/ppermute | solution.py:12
  549.8 3.3 bitcast_add_fusion
  553.1 4.2 convolution_bitcast_fusion.4
  557.6 89.9 %all-reduce.10.cloned.1.call-done = f32[256,256]{0,1:T(8,128)} async-done(((f32[256,256]{0,1:T(8,128)}), f32[256,256]{0,1:T(8,128)}) %all-reduce.10.cloned.1.call-update) | async-done | bytes 262160 | tf_op jit(solution)/shard_map/psum | solution.py:64
  647.5 1.5 collective-permute-start.2
  649.0 5.3 convolution_bitcast_fusion
  654.3 4.4 copy.107
  659.0 11.7 %cholesky.286 = f32[128,128]{1,0:T(8,128)S(1)} custom-call(f32[128,128]{1,0:T(8,128)S(1)} %cholesky.322), custom_call_target="Cholesky" | custom-call | tf_op jit(solution)/shard_map/jit(cholesky)/cholesky | solution.py:17
  670.8 9.8 %custom-call.36 = f32[1,128,128]{1,2,0:T(8,128)S(1)} custom-call(f32[1,128,128]{2,1,0:T(8,128)S(1)} %get-tuple-element.92), custom_call_target="InvertDiagBlocksLowerTriangular" | custom-call | tf_op jit(solution)/shard_map/jit(cholesky)/cholesky | solution.py:17
  681.1 11.9 %cholesky.303 = f32[128,128]{1,0:T(8,128)S(1)} custom-call(f32[128,128]{1,0:T(8,128)S(1)} %convolution_subtract_fusion.4), custom_call_target="Cholesky" | custom-call | tf_op jit(solution)/shard_map/jit(cholesky)/cholesky | solution.py:17
  695.7 4.0 while.7
  696.3 1.4 bitcast_dynamic-update-slice_fusion.8
  698.3 1.4 bitcast_dynamic-update-slice_fusion.8
  699.7 19.7 %custom-call.37 = f32[2,128,128]{1,2,0:T(8,128)S(1)} custom-call(f32[2,128,128]{2,1,0:T(8,128)S(1)} %get-tuple-element.29), custom_call_target="InvertDiagBlocksLowerTriangular" | custom-call | tf_op jit(solution)/shard_map/jit(_solve_triangular)/triangular_solve | solution.py:19
  720.3 3.7 convolution_bitcast_fusion.1
  724.0 2.5 copy.108
  (109 shorter events, 27.4 us)
Async XLA Ops:
  7.2 427.8 %copy-start = (f32[1,8,256,256]{3,2,1,0:T(8,128)S(1)}, f32[1,8,256,256]{3,2,1,0:T(8,128)}, u32[]{:S(2)}) copy-start(f32[1,8,256,256]{3,2,1,0:T(8,128)} %param.8) | copy-start | bytes 6291460
  7.2 97.7 %all-reduce.6.cloned.1.call-start = ((), (), s32[]{:S(2)}) async-start(), calls=%async_computation.2 | async-start | bytes 1048576 | tf_op jit(solution)/shard_map/psum | solution.py:26
  11.6 375.8 %all-reduce.8.cloned.1.call-start = ((), (), s32[]{:S(2)}) async-start(), calls=%async_computation.3 | async-start | bytes 524288 | tf_op jit(solution)/shard_map/psum | solution.py:40
  104.9 3.2 copy-start.6
  108.2 0.8 copy-start.7
  288.4 2.0 copy-start.2
  426.1 8.8 %collective-permute-start = (f32[256,256]{0,1:T(8,128)S(1)}, f32[256,256]{0,1:T(8,128)S(1)}, u32[]{:S(2)}, u32[]{:S(2)}) collective-permute-start(f32[256,256]{0,1:T(8,128)S(1)} %get-tuple-element.84), channel_id=1, source_target_pairs={{0,16},{16,0},{1,17},{17,1},{2,18},{18,2},{3,19},{19,3},{4,20},{20... | collective-permute-start | bytes 786440 | tf_op jit(solution)/shard_map/ppermute | solution.py:12
  434.9 1.9 copy-start.8
  439.8 54.9 %all-to-all-start.1 = ((f32[8,256,256]{2,0,1:T(8,128)}), f32[8,256,256]{2,0,1:T(8,128)S(1)}, u32[]{:S(2)}, u32[]{:S(2)}) async-start(f32[8,256,256]{2,0,1:T(8,128)} %copy.100), calls=%async_computation.1 | async-start | bytes 4194304 | tf_op jit(solution)/shard_map/all_to_all | solution.py:52
  443.6 204.0 %all-reduce.10.cloned.1.call-start = ((), (), s32[]{:S(2)}) async-start(), calls=%async_computation.4 | async-start | bytes 524288 | tf_op jit(solution)/shard_map/psum | solution.py:64
  498.3 2.6 copy-start.3
  498.3 5.0 copy-start.10
  498.3 5.0 copy-start.12
  498.3 5.4 copy-start.9
  500.8 3.7 copy-start.5
  500.8 48.9 %collective-permute-start.1 = (f32[128,16,256]{2,0,1:T(8,128)}, f32[128,16,256]{2,0,1:T(8,128)}, u32[]{:S(2)}, u32[]{:S(2)}) collective-permute-start(f32[128,16,256]{2,0,1:T(8,128)} %select_bitcast_fusion), channel_id=1, source_target_pairs={{0,16},{16,0},{1,17},{17,1},{2,18},{18,2},{3,19},{19,3},{4,20},{20... | collective-permute-start | bytes 6291464 | tf_op jit(solution)/shard_map/ppermute | solution.py:12
  553.1 4.2 copy-start.4
  647.5 11.2 %collective-permute-start.2 = (f32[256,256]{0,1:T(8,128)}, f32[256,256]{0,1:T(8,128)S(1)}, u32[]{:S(2)}, u32[]{:S(2)}) collective-permute-start(f32[256,256]{0,1:T(8,128)} %all-reduce.10.cloned.1.call-done), channel_id=1, source_target_pairs={{0,16},{16,0},{1,17},{17,1},{2,18},{18,2},{3,19},{19,3},{4,20},{20... | collective-permute-start | bytes 786440 | tf_op jit(solution)/shard_map/ppermute | solution.py:12
  654.3 4.5 copy-start.11
  720.3 7.1 copy-start.1
Sparse Core Ops, SparseCore 0:
  12.0 92.8 all-reduce.5
  298.0 89.3 all-reduce.7
  557.4 90.0 all-reduce.9
where the time goes:
time: 744 us; the launch traced here: 734 us
  waiting for transfers between devices  298 us (40%)
  other arithmetic  227 us (31%)
  blocking collectives  97.3 us (13%)
  matrix products  47.4 us (6%)
  local copies, waits for them, and re-layouts  37.8 us (5%)
  between operations  17.3 us (2%)
  starting transfers between devices  9.28 us (1%)
    another operation x23, other arithmetic, factored(): lower = jnp.linalg.cholesky(gram_matrix)  136 us
    all_to_all x1, blocking collectives, body(): lax.all_to_all(turned, 'row', split_axis=1, concat_axis=0, tiled=True)  97.3 us
    psum x1, waiting for transfers between devices, body(): leaf_grams = lax.psum(leaf_grams, 'row') / rows_total  93.2 us
    psum x1, waiting for transfers between devices, body(): row_total = lax.psum(two_gram, 'row')  89.9 us
    psum x1, waiting for transfers between devices, body(): one_gram = lax.psum(one_gram, 'row') / (rank_width * rank_width)  89.5 us
    another operation x5, other arithmetic, factored(): jax.scipy.linalg.solve_triangular(lower, identity, lower=True)  80.3 us
    ppermute x3, waiting for transfers between devices, swapped(): return lax.ppermute(value, axis, pairs)  25.7 us
  transfers between devices with their start and end apart: 7, of which 5 were waited for; matrix products, arithmetic and copies ran while one was open for 12% of the time, Pallas kernels for 0%

commit v1 on v0

v1 whole, which is shorter than its diff:
```python
import functools
import jax
import jax.numpy as jnp
from jax import lax
from jax.experimental import pallas as pl
from jax.experimental.pallas import tpu as pltpu
from jax.sharding import PartitionSpec as P

PRECISE = lax.Precision.HIGHEST
FAST = lax.Precision.HIGH
SUB = 8
LANE = 128


def swapped(value, axis, mask):
    pairs = [(source, source ^ mask) for source in range(lax.axis_size(axis))]
    return lax.ppermute(value, axis, pairs)


def pick(value, index):
    return lax.dynamic_index_in_dim(value, index, 0, keepdims=False)


def factor_kernel(scale, gram_ref, upper_ref, inverse_ref, work_ref):
    n = gram_ref.shape[0]
    work_ref[:, :n] = gram_ref[...] * scale
    row_ids = lax.broadcasted_iota(jnp.int32, (n, n), 0)
    col_ids = lax.broadcasted_iota(jnp.int32, (n, n), 1)
    work_ref[:, n:] = jnp.where(row_ids == col_ids, 1.0, 0.0)
    for start in range(0, n, SUB):
        first = (start // LANE) * LANE
        end = n + ((start + SUB + LANE - 1) // LANE) * LANE
        width = end - first
        offset = start - first
        panel = work_ref[start : start + SUB, first:end]
        rows = [jnp.broadcast_to(panel[i : i + 1, :], (SUB, width)) for i in range(SUB)]
        diag = {}
        for i in range(SUB):
            for j in range(i, SUB):
                entry = rows[i][:, offset + j : offset + j + 1]
                diag[i, j] = jnp.broadcast_to(entry, (SUB, LANE))
        sub_ids = lax.broadcasted_iota(jnp.int32, (SUB, width), 0)
        done = jnp.zeros((SUB, width), jnp.float32)
        for i in range(SUB):
            root = lax.rsqrt(diag[i, i])
            row = rows[i] * jnp.concatenate([root] * (width // LANE), axis=1)
            done = jnp.where(sub_ids == i, row, done)
            coef = {j: diag[i, j] * root for j in range(i + 1, SUB)}
            for j in range(i + 1, SUB):
                for l in range(j, SUB):
                    diag[j, l] = diag[j, l] - coef[j] * coef[l]
                rows[j] = rows[j] - jnp.concatenate([coef[j]] * (width // LANE), axis=1) * row
        lane_ids = lax.broadcasted_iota(jnp.int32, (SUB, width), 1)
        done = jnp.where(lane_ids >= offset + sub_ids, done, 0.0)
        if first:
            upper_ref[start : start + SUB, :first] = jnp.zeros((SUB, first), jnp.float32)
        upper_ref[start : start + SUB, first:] = done[:, : n - first]
        inverse_ref[start : start + SUB, : end - n] = done[:, n - first :]
        if end < 2 * n:
            inverse_ref[start : start + SUB, end - n :] = jnp.zeros((SUB, 2 * n - end), jnp.float32)
        below = start + SUB
        if below < n:
            left = (below // LANE) * LANE
            product = lax.dot_general(
                done[:, left - first : n - first],
                done[:, left - first :],
                (((0,), (0,)), ((), ())),
                precision=PRECISE,
                preferred_element_type=jnp.float32,
            )
            work_ref[below:, left:end] = work_ref[below:, left:end] - product[below - left :, :]


def factored(gram_matrix, scale):
    n = gram_matrix.shape[0]
    square = jax.ShapeDtypeStruct((n, n), jnp.float32)
    return pl.pallas_call(
        functools.partial(factor_kernel, scale),
        out_shape=(square, square),
        in_specs=[pl.BlockSpec(memory_space=pltpu.VMEM)],
        out_specs=(pl.BlockSpec(memory_space=pltpu.VMEM),) * 2,
        scratch_shapes=[pltpu.VMEM((n, 2 * n), jnp.float32)],
        compiler_params=pltpu.CompilerParams(vmem_limit_bytes=32 * 2**20),
        name="factor",
    )(gram_matrix)


def groups_of(size):
    return [list(range(0, size, 2)), list(range(1, size, 2))]


def scattered(value):
    size = lax.axis_size("row")
    core = lax.axis_index("row") % 2
    kept = pick(value, core) + swapped(pick(value, 1 - core), "row", 1)
    moved = lax.all_to_all(
        kept, "row", 0, 0, tiled=True, axis_index_groups=groups_of(size)
    )
    return moved.sum(0)


def collected(piece):
    size = lax.axis_size("row")
    core = lax.axis_index("row") % 2
    copies = jnp.broadcast_to(piece[None], (size // 2,) + piece.shape)
    own = lax.all_to_all(copies, "row", 0, 0, tiled=True, axis_index_groups=groups_of(size))
    other = swapped(own, "row", 1)
    return jnp.where(core == 0, jnp.stack([own, other]), jnp.stack([other, own]))


def pieces_of(gram):
    size = lax.axis_size("row")
    return gram.reshape(2, size // 2, -1, gram.shape[-1])


def body(leaves, level_one, level_two):
    rows = lax.axis_size("row")
    rank = leaves.shape[-1]
    node = lax.axis_index("node") % 2
    is_left = node == 0
    raw_two = level_two[0]
    sibling_two = swapped(raw_two, "node", 1)

    leaf_grams = jnp.einsum("nrc,nrd->ncd", leaves, leaves, precision=PRECISE)
    by_device = leaf_grams.reshape(2, 2, rows // 2, -1, rank).transpose(1, 2, 0, 3, 4)
    piece = scattered(by_device.reshape(2, rows // 2, -1, rank))
    full = collected(piece).reshape(2, rows // 2, 2, -1, rank).transpose(2, 0, 1, 3, 4)
    leaf_grams = full.reshape(2, rank, rank)
    leaf_scale = 1.0 / (leaves.shape[1] * rows)
    right_upper, right_inverse = factored(leaf_grams[1], leaf_scale)

    slab = level_one[0]
    depth = slab.shape[0]
    turned = jnp.einsum("jb,abk->ajk", right_upper, slab, precision=FAST)
    gathered = lax.all_to_all(turned, "row", split_axis=1, concat_axis=0, tiled=True)

    left_upper, left_inverse = factored(leaf_grams[0], leaf_scale)
    leaf_inverse = jnp.stack([left_inverse, right_inverse])
    leaf_bases = jnp.einsum("nrc,ndc->nrd", leaves, leaf_inverse, precision=FAST)

    moved_one = jnp.einsum("ia,ajk->ijk", left_upper, gathered, precision=FAST)
    flat_one = moved_one.reshape(-1, rank)
    one_gram = jnp.einsum("rc,rd->cd", flat_one, flat_one, precision=PRECISE)
    piece = scattered(pieces_of(one_gram))
    partner = swapped(piece, "node", 1)
    first = jnp.where(is_left, piece, partner)
    second = jnp.where(is_left, partner, piece)
    full = collected(jnp.stack([first, second])).transpose(2, 0, 1, 3, 4)
    one_grams = full.reshape(2, rank, rank)
    scale = 1.0 / (rank * rank)
    second_upper, second_inverse = factored(one_grams[1], scale)

    chosen = pick(second_upper.reshape(rows, 2, -1, rank).transpose(1, 0, 2, 3), node)
    chosen = chosen.reshape(-1, rank)
    pair = jnp.stack([raw_two, sibling_two], axis=1)
    pair = jnp.where(is_left, pair, pair[:, ::-1])
    pair = pair.reshape(-1, rank, rank)
    turned_two = jnp.einsum("jb,abk->ajk", chosen, pair, precision=FAST)
    gathered_two = lax.all_to_all(turned_two, "row", split_axis=1, concat_axis=0, tiled=True)

    first_upper, first_inverse = factored(one_grams[0], scale)
    one_inverse = jnp.where(is_left, first_inverse, second_inverse)
    level_one_bases = jnp.einsum("rc,dc->rd", flat_one, one_inverse, precision=FAST)
    level_one_bases = level_one_bases.reshape(moved_one.shape)[None]

    moved_two = jnp.einsum("ia,ajk->ijk", first_upper, gathered_two, precision=FAST)
    flat_two = moved_two.reshape(-1, rank)
    two_gram = jnp.einsum("rc,rd->cd", flat_two, flat_two, precision=PRECISE)
    by_parity = moved_two.reshape((rank // 2, 2) + moved_two.shape[1:])
    kept = jnp.where(is_left, by_parity[:, 0], by_parity[:, 1])
    sent = jnp.where(is_left, by_parity[:, 1], by_parity[:, 0])
    received = swapped(sent, "node", 1)
    piece = scattered(pieces_of(two_gram))
    piece = piece + swapped(piece, "node", 1)
    two_gram = collected(piece).reshape(rank, rank)
    two_upper, two_inverse = factored(two_gram, scale)
    whole_two = jnp.where(
        is_left,
        jnp.concatenate([kept, received], axis=1),
        jnp.concatenate([received, kept], axis=1),
    )
    level_two_bases = jnp.einsum("ijk,lk->ijl", whole_two, two_inverse, precision=FAST)[None]
    return (leaf_bases, level_one_bases, level_two_bases, two_upper[None])


def solution(mesh):
    placed = (P("node", "row", None), P("node", "row", None, None), P("node", "row", None, None))
    return jax.shard_map(
        body,
        mesh=mesh,
        in_specs=placed,
        out_specs=(
            P("node", "row", None),
            P("node", None, "row", None),
            P("node", None, "row", None),
            P("node", None, None),
        ),
        check_vma=False,
    )
```

time: 744 us -> 399 us (0.54)
  other arithmetic: 227 us -> 10.4 us
  waiting for transfers between devices: 298 us -> 96 us
  Pallas kernels: 0 us -> 104 us
  blocking collectives: 97.3 us -> 72.3 us
  starting transfers between devices: 9.28 us -> 31.1 us
  between operations: 17.3 us -> 1.21 us
  matrix products: 47.4 us -> 34.4 us
  local copies, waits for them, and re-layouts: 37.8 us -> 45.6 us
    psum x3 -> x0, waiting for transfers between devices: 273 us -> none  [the longest x1 93.2 us: body(): leaf_grams = lax.psum(leaf_grams, 'row') / rows_total]
    another operation x28 -> x3, other arithmetic: 217 us -> 4.58 us  [the longest x1 4.57 us: body(): pair = jnp.stack([raw_two, sibling_two], axis=1)]
    pallas_call x0 -> x5, Pallas kernels: none -> 104 us  [factored(): pl.pallas_call(functools.partial(factor_kernel, scale), out_shape=(square...]
    all_to_all x0 -> x3, waiting for transfers between devices: none -> 63.8 us  [the longest x1 55.4 us: body(): lax.all_to_all(turned, 'row', split_axis=1, concat_axis=0, tiled=True)]
    all_to_all x1 -> x4, blocking collectives: 97.3 us -> 72.3 us  [the longest x3 60.3 us: scattered(): lax.all_to_all(kept, 'row', 0, 0, tiled=True, axis_index_groups=groups_of...]
    all_to_all x1, waiting for transfers between devices: 0.01 us -> 20.5 us  [body(): lax.all_to_all(turned_two, 'row', split_axis=1, concat_axis=0, tiled=True)]
    all_to_all x0 -> x3, starting transfers between devices: none -> 19.3 us  [the longest x2 14.8 us: collected(): lax.all_to_all(copies, 'row', 0, 0, tiled=True, axis_index_groups=groups_...]
    dot_general x0 -> x4, local copies, waits for them, and re-layouts: none -> 15.5 us  [the longest x1 5.69 us: body(): one_gram = jnp.einsum('rc,rd->cd', flat_one, flat_one, precision=PRECISE)]
  transfers between devices with their start and end apart: 7 -> 14, of which waited for: 5 -> 9; matrix products, arithmetic and copies ran while one was open for 12% -> 12% of each run, Pallas kernels for 0% -> 16%
where the time goes in v1:
time: 399 us; the launch traced here: 395 us
  Pallas kernels  104 us (26%)
  waiting for transfers between devices  96 us (24%)
  blocking collectives  72.3 us (18%)
  local copies, waits for them, and re-layouts  45.6 us (11%)
  matrix products  34.4 us (9%)
  starting transfers between devices  31.1 us (8%)
  other arithmetic  10.4 us (3%)
    pallas_call x5, Pallas kernels, factored(): pl.pallas_call(functools.partial(factor_kernel, scale), out_shape=(square...  104 us
    all_to_all x3, blocking collectives, scattered(): lax.all_to_all(kept, 'row', 0, 0, tiled=True, axis_index_groups=groups_of...  60.3 us
    all_to_all x1, waiting for transfers between devices, body(): lax.all_to_all(turned, 'row', split_axis=1, concat_axis=0, tiled=True)  55.4 us
    all_to_all x1, waiting for transfers between devices, body(): lax.all_to_all(turned_two, 'row', split_axis=1, concat_axis=0, tiled=True)  20.5 us
    all_to_all x2, starting transfers between devices, collected(): lax.all_to_all(copies, 'row', 0, 0, tiled=True, axis_index_groups=groups_...  14.8 us
    all_to_all x1, blocking collectives, collected(): lax.all_to_all(copies, 'row', 0, 0, tiled=True, axis_index_groups=groups_...  12 us
    ppermute x10, waiting for transfers between devices, swapped(): return lax.ppermute(value, axis, pairs)  11.7 us
    unnamed x13, local copies, waits for them, and re-layouts  10.8 us
  transfers between devices with their start and end apart: 14, of which 9 were waited for; matrix products, arithmetic and copies ran while one was open for 12% of the time, Pallas kernels for 16%

profile of v1, /device:TPU:0, one launch (start us, length us, event | category | flops | bytes accessed | tf_op | source)
XLA Modules:
  0.0 395.1 jit_solution(8345444280388270513)
XLA Ops:
  1.9 1.9 fusion.38
  5.5 16.2 %all_to_all.66 = f32[8,32,256]{2,1,0:T(8,128)S(1)} all-to-all(f32[8,32,256]{2,1,0:T(8,128)S(1)} %bitcast_add_fusion), channel_id=1, replica_groups={{0,2,4,6,8,10,12,14},{1,3,5,7,9,11,13,15},{16,18,20,22,24,26,28,30},{17..., dimensions={0} | all-to-all | bytes 524288 | tf_op jit(solution)/shard_map/all_to_all | solution.py:96
  21.8 12.0 %all_to_all.67 = f32[8,32,256]{2,1,0:T(8,128)S(1)} all-to-all(f32[8,32,256]{2,1,0:T(8,128)S(1)} %broadcast_in_dim.10), channel_id=1, replica_groups={{0,2,4,6,8,10,12,14},{1,3,5,7,9,11,13,15},{16,18,20,22,24,26,28,30},{17..., dimensions={0} | all-to-all | bytes 524288 | tf_op jit(solution)/shard_map/all_to_all | solution.py:106
  33.8 1.5 collective-permute-done.1
  35.4 20.6 %factor.6 = (f32[256,256]{1,0:T(8,128)S(1)}, f32[256,256]{1,0:T(8,128)S(1)}) custom-call(f32[256,256]{1,0:T(8,128)S(1)} %bitcast.125), custom_call_target="tpu_custom_call" | custom-call | tf_op jit(solution)/shard_map/factor/pallas_call | solution.py:77
  56.0 4.6 %fusion.2 = f32[16,256,256]{2,1,0:T(8,128)S(1)} fusion(f32[1,16,256,256]{3,2,1,0:T(8,128)} %param.4, f32[256,256]{1,0:T(8,128)S(1)} %get-tuple-element.17), kind=kOutput, calls=%fused_computation.4 | convolution fusion | flops 1610612736 | bytes 8650752 | tf_op jit(solution)/shard_map/jb,abk->ajk/dot_general | solution.py:134
  60.6 4.4 %copy.49 = f32[16,256,256]{2,0,1:T(8,128)} copy(f32[16,256,256]{2,1,0:T(8,128)S(1)} %fusion.2) | data formatting | bytes 8388608 | tf_op jit(solution)/shard_map/jb,abk->ajk/transpose | solution.py:134
  65.1 4.6 %all-to-all-start.2 = ((f32[16,256,256]{2,0,1:T(8,128)}), f32[16,256,256]{2,0,1:T(8,128)}, u32[]{:S(2)}, u32[]{:S(2)}) async-start(f32[16,256,256]{2,0,1:T(8,128)} %copy.49), calls=%async_computation.2 | async-start | bytes 8388608 | tf_op jit(solution)/shard_map/all_to_all | solution.py:135
  69.6 1.6 collective-permute-start.5
  71.2 20.6 %factor.5 = (f32[256,256]{1,0:T(8,128)S(1)}, f32[256,256]{1,0:T(8,128)S(1)}) custom-call(f32[256,256]{1,0:T(8,128)S(1)} %bitcast.123), custom_call_target="tpu_custom_call" | custom-call | tf_op jit(solution)/shard_map/factor/pallas_call | solution.py:77
  91.8 55.4 %all-to-all-done.2 = f32[16,256,256]{2,0,1:T(8,128)} async-done(((f32[16,256,256]{2,0,1:T(8,128)}), f32[16,256,256]{2,0,1:T(8,128)}, u32[]{:S(2)}, u32[]{:S(2)}) %all-to-all-start.2) | async-done | bytes 4194336 | tf_op jit(solution)/shard_map/all_to_all | solution.py:135
  147.2 3.0 copy.50
  150.2 2.1 fusion.26
  152.3 4.4 %copy.51 = f32[256,16,256]{2,1,0:T(8,128)} copy(f32[256,16,256]{2,0,1:T(8,128)S(1)} %fusion.26) | data formatting | bytes 8388608 | tf_op jit(solution)/shard_map/ia,ajk->ijk/dot_general | solution.py:141
  156.7 5.7 %copy.52 = f32[256,4096]{1,0:T(8,128)} copy(f32[256,4096]{0,1:T(8,128)} %bitcast.130) | data formatting | bytes 8388608 | tf_op jit(solution)/shard_map/rc,rd->cd/dot_general | solution.py:143
  162.4 7.0 %fusion.39 = f32[2,8,16,256]{3,2,1,0:T(8,128)S(1)} fusion(f32[2,8,16,4096]{3,2,1,0:T(8,128)} %bitcast.134, f32[4096,256,1,1]{1,0,3,2:T(8,128)} %bitcast.131), kind=kOutput, calls=%fused_computation.58 | convolution fusion | flops 3221225472 | bytes 8650752 | tf_op jit(solution)/shard_map/rc,rd->cd/dot_general | solution.py:143
  171.3 26.3 %all_to_all.68 = f32[8,16,256]{2,1,0:T(8,128)S(1)} all-to-all(f32[8,16,256]{2,1,0:T(8,128)S(1)} %bitcast_add_fusion.2), channel_id=1, replica_groups={{0,2,4,6,8,10,12,14},{1,3,5,7,9,11,13,15},{16,18,20,22,24,26,28,30},{17..., dimensions={0} | all-to-all | bytes 262144 | tf_op jit(solution)/shard_map/all_to_all | solution.py:96
  197.7 1.6 collective-permute-start.3
  199.2 2.2 collective-permute-done.3
  202.2 3.8 all-to-all-start.4
  206.0 4.6 %pad_maximum_fusion = f32[8,2,256,256]{3,2,1,0:T(8,128)} fusion(f32[8,1,256,256]{3,2,1,0:T(8,128)} %bitcast.40, f32[8,1,256,256]{3,2,1,0:T(8,128)} %bitcast.142), kind=kLoop, calls=%fused_computation.1 | loop fusion | flops 1048576 | bytes 8388608 | tf_op jit(solution)/shard_map/stack | solution.py:155
  210.6 3.2 all-to-all-done.4
  213.8 4.1 %reverse_select_fusion = f32[8,2,256,256]{3,2,1,0:T(8,128)S(1)} fusion(f32[8,2,256,256]{3,2,1,0:T(8,128)} %pad_maximum_fusion, pred[]{:T(512)S(6)} %eq.17), kind=kLoop, calls=%fused_computation | loop fusion | flops 1048576 | bytes 8388609 | tf_op jit(solution)/shard_map/jit(_where)/select_n | solution.py:156
  218.0 20.8 %factor.8 = (f32[256,256]{1,0:T(8,128)S(1)}, f32[256,256]{1,0:T(8,128)S(1)}) custom-call(f32[256,256]{1,0:T(8,128)S(1)} %bitcast.126), custom_call_target="tpu_custom_call" | custom-call | tf_op jit(solution)/shard_map/factor/pallas_call | solution.py:77
  238.8 4.8 %convolution_bitcast_fusion.1 = f32[16,128,256]{1,2,0:T(8,128)} fusion(f32[16,256,256]{2,1,0:T(8,128)S(1)} %bitcast.132, f32[16,2,8,256]{3,2,1,0:T(8,128)S(1)} %bitcast.129, s32[]{:T(128)S(6)} %select_n.134), kind=kOutput, calls=%fused_computation.18 | convolution fusion | flops 805306368 | bytes 6422532 | tf_op jit(solution)/shard_map/jb,abk->ajk/dot_general | solution.py:158
  243.5 3.1 copy.54
  246.6 4.4 %all-to-all-start.5 = ((f32[16,128,256]{2,0,1:T(8,128)}), f32[16,128,256]{2,0,1:T(8,128)}, u32[]{:S(2)}, u32[]{:S(2)}) async-start(f32[16,128,256]{2,0,1:T(8,128)} %copy.54), calls=%async_computation.5 | async-start | bytes 4194304 | tf_op jit(solution)/shard_map/all_to_all | solution.py:159
  251.0 20.6 %factor.7 = (f32[256,256]{1,0:T(8,128)S(1)}, f32[256,256]{1,0:T(8,128)S(1)}) custom-call(f32[256,256]{1,0:T(8,128)S(1)} %bitcast.124), custom_call_target="tpu_custom_call" | custom-call | tf_op jit(solution)/shard_map/factor/pallas_call | solution.py:77
  271.6 20.5 %all-to-all-done.5 = f32[16,128,256]{2,0,1:T(8,128)} async-done(((f32[16,128,256]{2,0,1:T(8,128)}), f32[16,128,256]{2,0,1:T(8,128)}, u32[]{:S(2)}, u32[]{:S(2)}) %all-to-all-start.5) | async-done | bytes 2097184 | tf_op jit(solution)/shard_map/all_to_all | solution.py:159
  292.1 1.8 copy.56
  293.9 1.6 fusion.22
  295.5 1.3 copy-done.2
  296.8 2.5 copy.80
  299.3 3.4 reshape.81
  302.8 2.9 copy.60
  305.7 5.2 %fusion.11 = f32[2,8,16,256]{3,2,1,0:T(8,128)S(1)} fusion(f32[2,8,16,2048]{3,2,1,0:T(8,128)} %bitcast.136, f32[256,8,256]{2,0,1:T(8,128)} %copy-done.2), kind=kOutput, calls=%fused_computation.13 | convolution fusion | flops 1610612736 | bytes 4456448 | tf_op jit(solution)/shard_map/rc,rd->cd/dot_general | solution.py:168
  311.7 2.0 fusion.35
  313.8 1.5 select_bitcast_fusion.1
  315.3 1.5 collective-permute-start.6
  316.8 17.8 %all_to_all.69 = f32[8,16,256]{2,1,0:T(8,128)S(1)} all-to-all(f32[8,16,256]{2,1,0:T(8,128)S(1)} %bitcast_add_fusion.1), channel_id=1, replica_groups={{0,2,4,6,8,10,12,14},{1,3,5,7,9,11,13,15},{16,18,20,22,24,26,28,30},{17..., dimensions={0} | all-to-all | bytes 262144 | tf_op jit(solution)/shard_map/all_to_all | solution.py:96
  335.2 5.8 %collective-permute-done.8 = f32[16,256]{1,0:T(8,128)S(1)} collective-permute-done((f32[16,256]{1,0:T(8,128)S(1)}, f32[16,256]{1,0:T(8,128)S(1)}, u32[]{:S(2)}, u32[]{:S(2)}) %collective-permute-start.8) | collective-permute-done | bytes 16416 | tf_op jit(solution)/shard_map/ppermute | solution.py:17
  341.6 10.9 %all-to-all-start.7 = ((f32[8,16,256]{2,1,0:T(8,128)}), f32[8,16,256]{2,1,0:T(8,128)S(1)}, u32[]{:S(2)}, u32[]{:S(2)}) async-start(f32[8,16,256]{2,1,0:T(8,128)} %broadcast_in_dim.12), calls=%async_computation.7 | async-start | bytes 262144 | tf_op jit(solution)/shard_map/all_to_all | solution.py:106
  354.5 5.2 %all-to-all-done.7 = f32[8,16,256]{2,1,0:T(8,128)S(1)} async-done(((f32[8,16,256]{2,1,0:T(8,128)}), f32[8,16,256]{2,1,0:T(8,128)S(1)}, u32[]{:S(2)}, u32[]{:S(2)}) %all-to-all-start.7) | async-done | bytes 131104 | tf_op jit(solution)/shard_map/all_to_all | solution.py:106
  359.8 4.0 %convolution_bitcast_fusion = f32[1,256,16,256]{3,1,2,0:T(8,128)S(1)} fusion(f32[256,16,256]{2,0,1:T(8,128)} %copy-done.1, f32[256,256]{1,0:T(8,128)S(1)} %get-tuple-element.18, f32[256,256]{1,0:T(8,128)S(1)} %get-tuple-element.19, pred[]{:T(512)S(6)} %eq.17), kind=kOutput, calls=%fused_computation.5 | convolution fusion | flops 1610678272 | bytes 8912897 | tf_op jit(solution)/shard_map/rc,dc->rd/dot_general | solution.py:163
  363.8 4.4 %copy.62 = f32[1,256,16,256]{3,2,1,0:T(8,128)} copy(f32[1,256,16,256]{3,1,2,0:T(8,128)S(1)} %convolution_bitcast_fusion) | data formatting | bytes 8388608
  368.3 21.5 %factor.9 = (f32[256,256]{1,0:T(8,128)}, f32[256,256]{1,0:T(8,128)S(1)}) custom-call(f32[256,256]{1,0:T(8,128)S(1)} %bitcast.122), custom_call_target="tpu_custom_call" | custom-call | tf_op jit(solution)/shard_map/factor/pallas_call | solution.py:77
  389.8 2.6 fusion.14
  392.4 2.5 copy.63
  (46 shorter events, 9.9 us)
Async XLA Ops:
  0.6 1.2 copy-start
  3.8 1.7 collective-permute-start
  33.8 1.5 collective-permute-start.1
  65.1 82.2 %all-to-all-start.2 = ((f32[16,256,256]{2,0,1:T(8,128)}), f32[16,256,256]{2,0,1:T(8,128)}, u32[]{:S(2)}, u32[]{:S(2)}) async-start(f32[16,256,256]{2,0,1:T(8,128)} %copy.49), calls=%async_computation.2 | async-start | bytes 8388608 | tf_op jit(solution)/shard_map/all_to_all | solution.py:135
  69.6 136.4 %collective-permute-start.5 = (f32[8,256,256]{2,1,0:T(8,128)}, f32[8,256,256]{2,1,0:T(8,128)}, u32[]{:S(2)}, u32[]{:S(2)}) collective-permute-start(f32[8,256,256]{2,1,0:T(8,128)} %bitcast.141), channel_id=1, source_target_pairs={{0,16},{16,0},{1,17},{17,1},{2,18},{18,2},{3,19},{19,3},{4,20},{20... | collective-permute-start | bytes 6291464 | tf_op jit(solution)/shard_map/ppermute | solution.py:17
  152.3 4.4 %copy-start.1 = (f32[256,16,256]{2,0,1:T(8,128)}, f32[256,16,256]{2,0,1:T(8,128)S(1)}, u32[]{:S(2)}) copy-start(f32[256,16,256]{2,0,1:T(8,128)S(1)} %fusion.26) | copy-start | bytes 12582916
  169.4 1.8 collective-permute-start.2
  197.7 3.8 collective-permute-start.3
  202.2 11.6 %all-to-all-start.4 = ((f32[8,2,16,256]{3,2,1,0:T(8,128)}), f32[8,2,16,256]{3,2,1,0:T(8,128)S(1)}, u32[]{:S(2)}, u32[]{:S(2)}) async-start(f32[8,2,16,256]{3,2,1,0:T(8,128)} %broadcast_in_dim.11), calls=%async_computation.4 | async-start | bytes 524288 | tf_op jit(solution)/shard_map/all_to_all | solution.py:106
  213.8 4.1 %collective-permute-start.4 = (f32[8,2,16,256]{3,2,1,0:T(8,128)S(1)}, f32[8,2,16,256]{3,2,1,0:T(8,128)S(1)}, u32[]{:S(2)}, u32[]{:S(2)}) collective-permute-start(f32[8,2,16,256]{3,2,1,0:T(8,128)S(1)} %all-to-all-done.4), channel_id=1, source_target_pairs={{0,1},{1,0},{2,3},{3,2},{4,5},{5,4},{6,7},{7,6},{8,9},{9,8},{10,11... | collective-permute-start | bytes 786440 | tf_op jit(solution)/shard_map/ppermute | solution.py:17
  246.6 45.5 %all-to-all-start.5 = ((f32[16,128,256]{2,0,1:T(8,128)}), f32[16,128,256]{2,0,1:T(8,128)}, u32[]{:S(2)}, u32[]{:S(2)}) async-start(f32[16,128,256]{2,0,1:T(8,128)} %copy.54), calls=%async_computation.5 | async-start | bytes 4194304 | tf_op jit(solution)/shard_map/all_to_all | solution.py:159
  295.5 1.3 copy-start.2
  305.7 6.1 %copy-start.3 = (f32[128,2,8,256]{3,1,0,2:T(2,128)S(1)}, f32[128,2,8,256]{3,1,0,2:T(2,128)}, u32[]{:S(2)}) copy-start(f32[128,2,8,256]{3,1,0,2:T(2,128)} %reshape.81) | copy-start | bytes 6291460
  310.9 5.9 %collective-permute-start.7 = (f32[8,16,256]{2,1,0:T(8,128)S(1)}, f32[8,16,256]{2,1,0:T(8,128)S(1)}, u32[]{:S(2)}, u32[]{:S(2)}) collective-permute-start(f32[8,16,256]{2,1,0:T(8,128)S(1)} %dynamic-slice_bitcast_fusion.1), channel_id=1, source_target_pairs={{0,1},{1,0},{2,3},{3,2},{4,5},{5,4},{6,7},{7,6},{8,9},{9,8},{10,11... | collective-permute-start | bytes 393224 | tf_op jit(solution)/shard_map/ppermute | solution.py:17
  315.3 74.5 %collective-permute-start.6 = (f32[128,8,256]{2,0,1:T(8,128)}, f32[128,8,256]{2,0,1:T(8,128)}, u32[]{:S(2)}, u32[]{:S(2)}) collective-permute-start(f32[128,8,256]{2,0,1:T(8,128)} %get-tuple-element.41), channel_id=1, source_target_pairs={{0,16},{16,0},{1,17},{17,1},{2,18},{18,2},{3,19},{19,3},{4,20},{20... | collective-permute-start | bytes 3145736 | tf_op jit(solution)/shard_map/ppermute | solution.py:17
  334.6 6.4 %collective-permute-start.8 = (f32[16,256]{1,0:T(8,128)S(1)}, f32[16,256]{1,0:T(8,128)S(1)}, u32[]{:S(2)}, u32[]{:S(2)}) collective-permute-start(f32[16,256]{1,0:T(8,128)S(1)} %reduce_sum.29), channel_id=1, source_target_pairs={{0,16},{16,0},{1,17},{17,1},{2,18},{18,2},{3,19},{19,3},{4,20},{20... | collective-permute-start | bytes 49160 | tf_op jit(solution)/shard_map/ppermute | solution.py:17
  341.6 18.1 %all-to-all-start.7 = ((f32[8,16,256]{2,1,0:T(8,128)}), f32[8,16,256]{2,1,0:T(8,128)S(1)}, u32[]{:S(2)}, u32[]{:S(2)}) async-start(f32[8,16,256]{2,1,0:T(8,128)} %broadcast_in_dim.12), calls=%async_computation.7 | async-start | bytes 262144 | tf_op jit(solution)/shard_map/all_to_all | solution.py:106
  359.8 8.5 %collective-permute-start.9 = (f32[8,16,256]{2,1,0:T(8,128)S(1)}, f32[8,16,256]{2,1,0:T(8,128)S(1)}, u32[]{:S(2)}, u32[]{:S(2)}) collective-permute-start(f32[8,16,256]{2,1,0:T(8,128)S(1)} %all-to-all-done.7), channel_id=1, source_target_pairs={{0,1},{1,0},{2,3},{3,2},{4,5},{5,4},{6,7},{7,6},{8,9},{9,8},{10,11... | collective-permute-start | bytes 393224 | tf_op jit(solution)/shard_map/ppermute | solution.py:17
  363.8 26.0 %copy-start.4 = (f32[128,8,256]{2,0,1:T(8,128)S(1)}, f32[128,8,256]{2,0,1:T(8,128)}, u32[]{:S(2)}) copy-start(f32[128,8,256]{2,0,1:T(8,128)} %get-tuple-element.40) | copy-start | bytes 3145732
